TPU v7x, 32 devices: a whole 2x2x4 slice. The times are simulated.
32 devices in a mesh: run: 4 (over z), feat: 2 (over core), vox: 4 (over y, x).
Axes of the slice: x: 2, y: 2, z: 4, core: 2. Of those that a mesh axis runs over, the one named last changes fastest.
Arguments:
- stimulus: bfloat16 [4, 512, 256], P('run', None, 'feat')
- responses: bfloat16 [4, 512, 512], P('run', None, 'vox')
- run_lengths: int32 [4], P('run'), may hold values from 1 to 512, 1536 in all
- lag_steps: int32 [4], replicated, may hold values from 0 to 7, as said below
- ridge_grid: float32 [16], replicated, may hold values from 0.05 to 5
- ridge_pick: int32 [4, 2], P('run'), may hold values from 0 to 15
Outputs:
- weights: float32 [4, 2, 1024, 512], P('run', None, 'feat', 'vox')
- fold_errors: float32 [4, 2, 512], P('run', None, 'vox')
Inputs may be any that keep to these rules, and one draw needn't show every extreme that they name: lag_steps[j] is 2 j or 2 j + 1; lag_steps[0] is 0 and the last entry is 7.
All inputs are finite; a program needn't handle non-finite values. No bound on the sum of `run_lengths` on one device may be relied on, other than what follows from the above.
Results may differ from a plain program's by a relative error of at most 0.0003.
Values may be sent and summed in bfloat16 or wider, within the bound.
A program may use at most 128 MiB of HBM per device.

v0:
```python
import jax
import jax.numpy as jnp
from jax import lax
from jax.sharding import PartitionSpec as P


def carried_in(part, axis, combine, identity, reverse):
    count = lax.axis_size(axis)
    place = lax.axis_index(axis)
    ahead = count - 1 - place if reverse else place
    gathered = jax.tree.map(lambda a: lax.all_gather(a, axis), part)
    state = jax.tree.map(lambda a, e: jnp.zeros_like(a) + jnp.asarray(e, a.dtype), part, identity)

    def one(hop, state):
        source = count - 1 - hop if reverse else hop
        return combine(
            state, jax.tree.map(lambda a: lax.dynamic_index_in_dim(a, source, 0, False), gathered)
        )

    return lax.fori_loop(0, ahead, one, state)


def build_features(stim_run, lag_steps, length):
    count_t = stim_run.shape[0]
    steps_t = jnp.arange(count_t, dtype=jnp.int32)
    pieces = []
    for j in range(lag_steps.shape[0]):
        lag = lag_steps[j]
        shifted = jnp.roll(stim_run, lag, axis=0)
        keep = (steps_t >= lag) & (steps_t < length)
        pieces.append(jnp.where(keep[:, None], shifted, jnp.zeros_like(shifted)))
    stacked = jnp.stack(pieces, axis=2)
    return stacked.reshape(count_t, stim_run.shape[1] * lag_steps.shape[0])


def add_terms(first, second):
    return tuple((left + right for left, right in zip(first, second)))


def solve_fold(full_gram, full_cross, count, penalty, feats, masked, length):
    width = full_gram.shape[0]
    eye = jnp.eye(width, dtype=jnp.float32)
    cross_s = full_cross / count
    feats_wide = feats.astype(jnp.float32)
    target_wide = masked.astype(jnp.float32)

    def one_penalty(value):
        system = full_gram / count + value * eye
        lower = jnp.linalg.cholesky(system)
        inner = lax.linalg.triangular_solve(
            lower, cross_s, left_side=True, lower=True, transpose_a=False
        )
        solved = lax.linalg.triangular_solve(
            lower, inner, left_side=True, lower=True, transpose_a=True
        )
        predicted = jnp.dot(feats_wide, solved, precision=lax.Precision.HIGHEST)
        errors = jnp.sum((target_wide - predicted) ** 2, axis=0) / length.astype(jnp.float32)
        return (solved, errors)

    return lax.map(one_penalty, penalty)


def look_up(picks, ridge_grid):
    table_ids = jnp.arange(ridge_grid.shape[0], dtype=jnp.int32)
    hits = picks[:, None] == table_ids[None, :]
    return jnp.sum(
        jnp.where(hits, ridge_grid[None, :], jnp.zeros_like(ridge_grid)[None, :]), axis=1
    )


def local(stimulus, responses, run_lengths, lag_steps, ridge_grid, ridge_pick):
    whole = lax.all_gather(stimulus, "feat", axis=2, tiled=True)
    length = run_lengths[0]
    feats = build_features(whole[0], lag_steps, length)
    count_feat = lax.axis_size("feat")
    count_vox = lax.axis_size("vox")
    width = feats.shape[1]
    half = width // count_feat
    quarter = width // count_vox
    own_rows = lax.dynamic_slice_in_dim(feats, lax.axis_index("feat") * half, half, 1)
    columns = lax.dynamic_slice_in_dim(feats, lax.axis_index("vox") * quarter, quarter, 1)
    steps_t = jnp.arange(feats.shape[0], dtype=jnp.int32)
    masked = jnp.where((steps_t < length)[:, None], responses[0], jnp.zeros_like(responses[0]))
    contract = (((0,), (0,)), ((), ()))
    gram = lax.dot_general(own_rows, columns, contract, preferred_element_type=jnp.float32)
    cross = lax.dot_general(own_rows, masked, contract, preferred_element_type=jnp.float32)
    count = length.astype(jnp.float32).reshape(1)
    zeros = (jnp.zeros_like(gram), jnp.zeros_like(cross), jnp.zeros_like(count))
    before = carried_in((gram, cross, count), "run", add_terms, zeros, False)
    after = carried_in((gram, cross, count), "run", add_terms, zeros, True)
    rest_gram, rest_cross, rest_count = add_terms(before, after)
    wide_rows = lax.all_gather(rest_gram, "vox", axis=1, tiled=True)
    full_gram, full_cross = (
        lax.all_gather(wide_rows, "feat", axis=0, tiled=True),
        lax.all_gather(rest_cross, "feat", axis=0, tiled=True),
    )
    picks = ridge_pick[0]
    solved, errors = solve_fold(
        full_gram, full_cross, rest_count[0], look_up(picks, ridge_grid), feats, masked, length
    )
    kept = lax.dynamic_slice_in_dim(solved, lax.axis_index("feat") * half, half, 1)
    return (kept[None], errors[None])


def solution(mesh):
    return jax.shard_map(
        local,
        mesh=mesh,
        in_specs=(
            P("run", None, "feat"),
            P("run", None, "vox"),
            P("run"),
            P(),
            P(),
            P("run", None),
        ),
        out_specs=(P("run", None, "feat", "vox"), P("run", None, "vox")),
        check_vma=False,
    )
```

profile of v0, /device:TPU:0, one launch (start us, length us, event | category | flops | bytes accessed | tf_op | source)
XLA Modules:
  0.0 881.4 jit_solution(4735311009072833869)
XLA Ops:
  29.7 13.4 %all-reduce.1 = f32[4]{0:T(128)S(1)} all-reduce(f32[4]{0:T(128)S(1)} %dynamic-update-slice.75), channel_id=1, replica_groups=mesh['run'=4,'feat'=2,'vox'=4] {'run'}, use_global_device_ids=true, to_apply=%add.1 | all-reduce | flops 4 | bytes 32
  43.1 14.8 %all-gather.13.cloned.1.call-done = f32[2048,128]{1,0:T(8,128)} async-done(((f32[512,128]{1,0:T(8,128)}), f32[2048,128]{1,0:T(8,128)}) %all-gather.13.cloned.1.call-update) | async-done | bytes 1048592 | tf_op jit(solution)/shard_map/all_gather | solution.py:11
  57.9 47.5 %all-gather.11.cloned.1.call-done = f32[2048,256]{1,0:T(8,128)} async-done(((f32[512,256]{1,0:T(8,128)}), f32[2048,256]{1,0:T(8,128)}) %all-gather.11.cloned.1.call-update) | async-done | bytes 2097168 | tf_op jit(solution)/shard_map/all_gather | solution.py:11
  105.5 10.3 %while.49 = (s32[]{:T(128)}, f32[512,256]{1,0:T(8,128)S(1)}, f32[512,128]{1,0:T(8,128)S(1)}, f32[1]{0:T(128)}, s32[]{:T(128)}, /*index=5*/f32[4,512,256]{2,1,0:T...) while((s32[]{:T(128)}, f32[512,256]{1,0:T(8,128)S(1)}, ...), condition=%wide.region_4.6_spmd, body=%wide.region_3.5_spmd.sunk | while | flops 196615 | bytes 2359491 | solution.py:20
  117.3 34.1 %all-gather.7.cloned.1.call-done = f32[512,1024]{0,1:T(8,128)} async-done(((f32[512,256]{0,1:T(8,128)}), f32[512,1024]{0,1:T(8,128)}) %all-gather.7.cloned.1.call-update) | async-done | bytes 2097168 | tf_op jit(solution)/shard_map/all_gather | solution.py:92
  155.5 11.1 %all-gather.9.cloned.1.call-done = f32[1024,1024]{0,1:T(8,128)} async-done(((f32[512,1024]{0,1:T(8,128)}), f32[1024,1024]{0,1:T(8,128)}) %all-gather.9.cloned.1.call-update) | async-done | bytes 4194320 | tf_op jit(solution)/shard_map/all_gather | solution.py:94
  166.5 706.2 %while.51 = (s32[]{:T(128)}, f32[2,1024,128]{2,1,0:T(8,128)}, f32[2,128]{1,0:T(2,128)S(1)}, f32[]{:T(128)}, f32[1024,1024]{0,1:T(8,128)}, /*index=5*/f32[2]{0:T(...) while((s32[]{:T(128)}, f32[2,1024,128]{2,1,0:T(8,128)}, ...), condition=%wide.region_23.25_spmd.clone, body=%wide.region_5.24_spmd.clone.sunk | while | flops 5452662272 | bytes 122106424 | solution.py:60
  185.5 11.7 %cholesky.1066 = f32[128,128]{1,0:T(8,128)S(1)} custom-call(f32[128,128]{1,0:T(8,128)S(1)} %cholesky.1065), custom_call_target="Cholesky" | custom-call | tf_op jit(solution)/shard_map/while/body/eval_jaxpr/jit(cholesky)/cholesky | solution.py:49
  197.2 9.8 %custom-call.140 = f32[1,128,128]{1,2,0:T(8,128)S(1)} custom-call(f32[1,128,128]{2,1,0:T(8,128)S(1)} %get-tuple-element.722), custom_call_target="InvertDiagBlocksLowerTriangular" | custom-call | tf_op jit(solution)/shard_map/while/body/eval_jaxpr/jit(cholesky)/cholesky | solution.py:49
  213.5 12.3 %cholesky.1069 = f32[128,128]{1,0:T(8,128)S(1)} custom-call(f32[128,128]{1,0:T(8,128)S(1)} %cholesky.1068), custom_call_target="Cholesky" | custom-call | tf_op jit(solution)/shard_map/while/body/eval_jaxpr/jit(cholesky)/cholesky | solution.py:49
  228.2 9.8 %custom-call.141 = f32[1,128,128]{1,2,0:T(8,128)S(1)} custom-call(f32[1,128,128]{2,1,0:T(8,128)S(1)} %get-tuple-element.726), custom_call_target="InvertDiagBlocksLowerTriangular" | custom-call | tf_op jit(solution)/shard_map/while/body/eval_jaxpr/jit(cholesky)/cholesky | solution.py:49
  241.4 11.7 %cholesky.1071 = f32[128,128]{1,0:T(8,128)S(1)} custom-call(f32[128,128]{1,0:T(8,128)S(1)} %cholesky.1070), custom_call_target="Cholesky" | custom-call | tf_op jit(solution)/shard_map/while/body/eval_jaxpr/jit(cholesky)/cholesky | solution.py:49
  268.4 11.9 %cholesky.1073 = f32[128,128]{1,0:T(8,128)S(1)} custom-call(f32[128,128]{1,0:T(8,128)S(1)} %cholesky.1072), custom_call_target="Cholesky" | custom-call | tf_op jit(solution)/shard_map/while/body/eval_jaxpr/jit(cholesky)/cholesky | solution.py:49
  295.5 11.7 %cholesky.1075 = f32[128,128]{1,0:T(8,128)S(1)} custom-call(f32[128,128]{1,0:T(8,128)S(1)} %cholesky.1074), custom_call_target="Cholesky" | custom-call | tf_op jit(solution)/shard_map/while/body/eval_jaxpr/jit(cholesky)/cholesky | solution.py:49
  309.2 10.0 %custom-call.144 = f32[1,128,128]{1,2,0:T(8,128)S(1)} custom-call(f32[1,128,128]{2,1,0:T(8,128)S(1)} %get-tuple-element.732), custom_call_target="InvertDiagBlocksLowerTriangular" | custom-call | tf_op jit(solution)/shard_map/while/body/eval_jaxpr/jit(cholesky)/cholesky | solution.py:49
  322.5 11.7 %cholesky.1077 = f32[128,128]{1,0:T(8,128)S(1)} custom-call(f32[128,128]{1,0:T(8,128)S(1)} %cholesky.1076), custom_call_target="Cholesky" | custom-call | tf_op jit(solution)/shard_map/while/body/eval_jaxpr/jit(cholesky)/cholesky | solution.py:49
  348.9 12.1 %cholesky.1079 = f32[128,128]{1,0:T(8,128)S(1)} custom-call(f32[128,128]{1,0:T(8,128)S(1)} %cholesky.1078), custom_call_target="Cholesky" | custom-call | tf_op jit(solution)/shard_map/while/body/eval_jaxpr/jit(cholesky)/cholesky | solution.py:49
  375.4 11.7 %cholesky.1080 = f32[128,128]{1,0:T(8,128)S(1)} custom-call(f32[128,128]{1,0:T(8,128)S(1)} %convolution_subtract_fusion.48), custom_call_target="Cholesky" | custom-call | tf_op jit(solution)/shard_map/while/body/eval_jaxpr/jit(cholesky)/cholesky | solution.py:49
  393.9 27.4 %while.52 = (s32[]{:T(128)}, f32[1024,1024]{1,0:T(8,128)}, s32[8,2]{0,1:T(2,128)S(1)}, f32[8,128,128]{2,1,0:T(8,128)}, s32[]{:T(128)}) while((s32[]{:T(128)}, f32[1024,1024]{1,0:T(8,128)}, s32[8,2]{0,1:T(2,128)S(1)}, f32[8,128,128]{2,1,0:T(8,128)}, s32[]{:T(128)}) %tuple.173), condition=%wide.while_cond, body=%wide.while_body.sunk | while | flops 2 | bytes 132705 | solution.py:53
  421.3 79.6 %custom-call.148 = f32[8,128,128]{1,2,0:T(8,128)S(1)} custom-call(f32[8,128,128]{2,1,0:T(8,128)} %get-tuple-element.748), custom_call_target="InvertDiagBlocksLowerTriangular" | custom-call | tf_op jit(solution)/shard_map/while/body/eval_jaxpr/triangular_solve | solution.py:53
  538.2 11.7 %cholesky.1066 = f32[128,128]{1,0:T(8,128)S(1)} custom-call(f32[128,128]{1,0:T(8,128)S(1)} %cholesky.1065), custom_call_target="Cholesky" | custom-call | tf_op jit(solution)/shard_map/while/body/eval_jaxpr/jit(cholesky)/cholesky | solution.py:49
  549.9 9.8 %custom-call.140 = f32[1,128,128]{1,2,0:T(8,128)S(1)} custom-call(f32[1,128,128]{2,1,0:T(8,128)S(1)} %get-tuple-element.722), custom_call_target="InvertDiagBlocksLowerTriangular" | custom-call | tf_op jit(solution)/shard_map/while/body/eval_jaxpr/jit(cholesky)/cholesky | solution.py:49
  566.2 11.9 %cholesky.1069 = f32[128,128]{1,0:T(8,128)S(1)} custom-call(f32[128,128]{1,0:T(8,128)S(1)} %cholesky.1068), custom_call_target="Cholesky" | custom-call | tf_op jit(solution)/shard_map/while/body/eval_jaxpr/jit(cholesky)/cholesky | solution.py:49
  593.7 11.7 %cholesky.1071 = f32[128,128]{1,0:T(8,128)S(1)} custom-call(f32[128,128]{1,0:T(8,128)S(1)} %cholesky.1070), custom_call_target="Cholesky" | custom-call | tf_op jit(solution)/shard_map/while/body/eval_jaxpr/jit(cholesky)/cholesky | solution.py:49
  620.7 11.9 %cholesky.1073 = f32[128,128]{1,0:T(8,128)S(1)} custom-call(f32[128,128]{1,0:T(8,128)S(1)} %cholesky.1072), custom_call_target="Cholesky" | custom-call | tf_op jit(solution)/shard_map/while/body/eval_jaxpr/jit(cholesky)/cholesky | solution.py:49
  647.8 11.7 %cholesky.1075 = f32[128,128]{1,0:T(8,128)S(1)} custom-call(f32[128,128]{1,0:T(8,128)S(1)} %cholesky.1074), custom_call_target="Cholesky" | custom-call | tf_op jit(solution)/shard_map/while/body/eval_jaxpr/jit(cholesky)/cholesky | solution.py:49
  661.5 10.2 %custom-call.144 = f32[1,128,128]{1,2,0:T(8,128)S(1)} custom-call(f32[1,128,128]{2,1,0:T(8,128)S(1)} %get-tuple-element.732), custom_call_target="InvertDiagBlocksLowerTriangular" | custom-call | tf_op jit(solution)/shard_map/while/body/eval_jaxpr/jit(cholesky)/cholesky | solution.py:49
  675.0 11.7 %cholesky.1077 = f32[128,128]{1,0:T(8,128)S(1)} custom-call(f32[128,128]{1,0:T(8,128)S(1)} %cholesky.1076), custom_call_target="Cholesky" | custom-call | tf_op jit(solution)/shard_map/while/body/eval_jaxpr/jit(cholesky)/cholesky | solution.py:49
  701.4 11.9 %cholesky.1079 = f32[128,128]{1,0:T(8,128)S(1)} custom-call(f32[128,128]{1,0:T(8,128)S(1)} %cholesky.1078), custom_call_target="Cholesky" | custom-call | tf_op jit(solution)/shard_map/while/body/eval_jaxpr/jit(cholesky)/cholesky | solution.py:49
  727.7 11.7 %cholesky.1080 = f32[128,128]{1,0:T(8,128)S(1)} custom-call(f32[128,128]{1,0:T(8,128)S(1)} %convolution_subtract_fusion.48), custom_call_target="Cholesky" | custom-call | tf_op jit(solution)/shard_map/while/body/eval_jaxpr/jit(cholesky)/cholesky | solution.py:49
  746.2 27.4 %while.52 = (s32[]{:T(128)}, f32[1024,1024]{1,0:T(8,128)}, s32[8,2]{0,1:T(2,128)S(1)}, f32[8,128,128]{2,1,0:T(8,128)}, s32[]{:T(128)}) while((s32[]{:T(128)}, f32[1024,1024]{1,0:T(8,128)}, s32[8,2]{0,1:T(2,128)S(1)}, f32[8,128,128]{2,1,0:T(8,128)}, s32[]{:T(128)}) %tuple.173), condition=%wide.while_cond, body=%wide.while_body.sunk | while | flops 2 | bytes 132705 | solution.py:53
  773.6 79.6 %custom-call.148 = f32[8,128,128]{1,2,0:T(8,128)S(1)} custom-call(f32[8,128,128]{2,1,0:T(8,128)} %get-tuple-element.748), custom_call_target="InvertDiagBlocksLowerTriangular" | custom-call | tf_op jit(solution)/shard_map/while/body/eval_jaxpr/triangular_solve | solution.py:53
  (336 shorter events, 324.6 us)
Async XLA Ops:
  7.2 18.7 %copy-start.5 = (bf16[1,512,128]{2,1,0:T(8,128)(2,1)S(1)}, bf16[1,512,128]{2,1,0:T(8,128)(2,1)}, u32[]{:S(2)}) copy-start(bf16[1,512,128]{2,1,0:T(8,128)(2,1)} %param.15) | copy-start | bytes 393220
  7.2 50.7 %all-gather.13.cloned.1.call-start = ((), (), s32[]{:S(2)}) async-start(), calls=%async_computation.3 | async-start | bytes 1310720 | tf_op jit(solution)/shard_map/all_gather | solution.py:11
  24.5 3.8 copy-start.9
  25.8 79.6 %copy-start.2 = (bf16[512,1024]{0,1:T(8,128)(2,1)}, bf16[512,1024]{0,1:T(8,128)(2,1)S(1)}, u32[]{:S(2)}) copy-start(bf16[512,1024]{0,1:T(8,128)(2,1)S(1)} %reshape.193) | copy-start | bytes 3145732
  27.1 78.3 %all-gather.11.cloned.1.call-start = ((), (), s32[]{:S(2)}) async-start(), calls=%async_computation.2 | async-start | bytes 2621440 | tf_op jit(solution)/shard_map/all_gather | solution.py:11
  28.3 123.2 %all-gather.7.cloned.1.call-start = ((), (), s32[]{:S(2)}) async-start(), calls=%async_computation | async-start | bytes 2621440 | tf_op jit(solution)/shard_map/all_gather | solution.py:92
  116.1 36.9 %copy-start.7 = (f32[16]{0:T(128)S(1)}, f32[16]{0:T(128)}, u32[]{:S(2)}) copy-start(f32[16]{0:T(128)} %param.18) | copy-start | bytes 196
  116.1 36.9 %copy-start.8 = (s32[1,2]{1,0:T(1,128)S(1)}, s32[1,2]{1,0:T(1,128)}, u32[]{:S(2)}) copy-start(s32[1,2]{1,0:T(1,128)} %param.19) | copy-start | bytes 28
  117.2 49.3 %all-gather.9.cloned.1.call-start = ((), (), s32[]{:S(2)}) async-start(), calls=%async_computation.1 | async-start | bytes 6291456 | tf_op jit(solution)/shard_map/all_gather | solution.py:94
  183.5 2.0 copy-start.1
  500.9 8.2 copy-start
  511.8 5.2 copy-start.3
  517.1 2.0 copy-start.4
  536.2 2.0 copy-start.1
  853.2 8.2 copy-start
  864.2 5.2 copy-start.3
  869.4 2.0 copy-start.4
  872.7 1.9 copy-start.6
Sparse Core Ops, SparseCore 0:
  27.2 30.6 all-gather.12
  60.0 45.3 all-gather.10
  117.4 34.0 all-gather.6
  152.8 13.6 all-gather.8
where the time goes:
time: 888 us; the launch traced here: 881 us
  other arithmetic  548 us (62%)
  waiting for transfers between devices  108 us (12%)
  local copies, waits for them, and re-layouts  86 us (10%)
  matrix products  83.5 us (9%)
  between operations  22.6 us (3%)
  blocking collectives  17.9 us (2%)
  loops' own time  15.6 us (2%)
    another operation x60, other arithmetic, one_penalty(): lower = jnp.linalg.cholesky(system)  345 us
    another operation x6, other arithmetic, one_penalty(): lax.linalg.triangular_solve(lower, inner, left_side=True, lower=True, tra...  169 us
    all_gather x2, waiting for transfers between devices, carried_in(): gathered = jax.tree.map(lambda a: lax.all_gather(a, axis), part)  62.3 us
    another operation x48, local copies, waits for them, and re-layouts  54.7 us
    another operation x28, matrix products, one_penalty(): lower = jnp.linalg.cholesky(system)  46.2 us
    all_gather x1, waiting for transfers between devices, local(): wide_rows = lax.all_gather(rest_gram, 'vox', axis=1, tiled=True)  34.1 us
    another operation x30, matrix products, one_penalty(): lax.linalg.triangular_solve(lower, cross_s, left_side=True, lower=True, t...  19.5 us
  transfers between devices with their start and end apart: 4, of which 4 were waited for; matrix products, arithmetic and copies ran while one was open for 0% of the time, Pallas kernels for 0%

commit v1 on v0

--- a/solution.py
+++ b/solution.py
@@ -2,6 +2,12 @@
 import jax.numpy as jnp
 from jax import lax
 from jax.sharding import PartitionSpec as P
+
+
+def joined_along(blocks, dim):
+    shape = list(blocks.shape[1:])
+    shape[dim] *= blocks.shape[0]
+    return jnp.moveaxis(blocks, 0, dim).reshape(shape)
 
 
 def carried_in(part, axis, combine, identity, reverse):
@@ -89,7 +95,19 @@
     before = carried_in((gram, cross, count), "run", add_terms, zeros, False)
     after = carried_in((gram, cross, count), "run", add_terms, zeros, True)
     rest_gram, rest_cross, rest_count = add_terms(before, after)
-    wide_rows = lax.all_gather(rest_gram, "vox", axis=1, tiled=True)
+    peers = lax.axis_size("vox")
+    pairs = [(i, (i + 1) % peers) for i in range(peers)]
+    back = [(b, a_2) for a_2, b in pairs]
+    lower_2, upper = ([], [])
+    for step in range(peers - 1):
+        if step % 2 == 0:
+            lower_2.append(lax.ppermute(lower_2[-1] if lower_2 else rest_gram, "vox", pairs))
+        else:
+            upper.append(lax.ppermute(upper[-1] if upper else rest_gram, "vox", back))
+    tiles = jnp.stack([*lower_2[::-1], rest_gram, *upper])
+    shift = lax.axis_index("vox") - len(lower_2)
+    tiles = tiles[(jnp.arange(peers) - shift) % peers]
+    wide_rows = joined_along(tiles, 1)
     full_gram, full_cross = (
         lax.all_gather(wide_rows, "feat", axis=0, tiled=True),
         lax.all_gather(rest_cross, "feat", axis=0, tiled=True),

time: 888 us -> 894 us (level)
    all_gather x1 -> x0, waiting for transfers between devices: 34.1 us -> none  [local(): wide_rows = lax.all_gather(rest_gram, 'vox', axis=1, tiled=True)]
    ppermute x0 -> x3, waiting for transfers between devices: none -> 33.5 us  [the longest x2 22.9 us: local(): lax.ppermute(lower_2[-1] if lower_2 else rest_gram, 'vox', pairs)]
  transfers between devices with their start and end apart: 4 -> 6, of which waited for: 4 -> 6; matrix products, arithmetic and copies ran while one was open for 0% -> 0% of each run, Pallas kernels for 0% -> 0%
where the time goes in v1:
time: 894 us; the launch traced here: 887 us
  other arithmetic  549 us (61%)
  waiting for transfers between devices  104 us (12%)
  local copies, waits for them, and re-layouts  91.4 us (10%)
  matrix products  83.4 us (9%)
  between operations  22.5 us (3%)
  blocking collectives  17.9 us (2%)
  loops' own time  15.6 us (2%)
    another operation x60, other arithmetic, one_penalty(): lower = jnp.linalg.cholesky(system)  345 us
    another operation x6, other arithmetic, one_penalty(): lax.linalg.triangular_solve(lower, inner, left_side=True, lower=True, tra...  169 us
    all_gather x2, waiting for transfers between devices, carried_in(): gathered = jax.tree.map(lambda a: lax.all_gather(a, axis), part)  62.3 us
    another operation x48, local copies, waits for them, and re-layouts  54.7 us
    another operation x28, matrix products, one_penalty(): lower = jnp.linalg.cholesky(system)  46.2 us
    ppermute x2, waiting for transfers between devices, local(): lax.ppermute(lower_2[-1] if lower_2 else rest_gram, 'vox', pairs)  22.9 us
    another operation x30, matrix products, one_penalty(): lax.linalg.triangular_solve(lower, cross_s, left_side=True, lower=True, t...  19.5 us
  transfers between devices with their start and end apart: 6, of which 6 were waited for; matrix products, arithmetic and copies ran while one was open for 0% of the time, Pallas kernels for 0%

profile of v1, /device:TPU:0, one launch (start us, length us, event | category | flops | bytes accessed | tf_op | source)
XLA Modules:
  0.0 887.1 jit_solution(1703808115321104832)
XLA Ops:
  29.7 13.4 %all-reduce.1 = f32[4]{0:T(128)S(1)} all-reduce(f32[4]{0:T(128)S(1)} %dynamic-update-slice.75), channel_id=1, replica_groups=mesh['run'=4,'feat'=2,'vox'=4] {'run'}, use_global_device_ids=true, to_apply=%add.1 | all-reduce | flops 4 | bytes 32
  43.1 14.8 %all-gather.10.cloned.1.call-done = f32[2048,128]{1,0:T(8,128)} async-done(((f32[512,128]{1,0:T(8,128)}), f32[2048,128]{1,0:T(8,128)}) %all-gather.10.cloned.1.call-update) | async-done | bytes 1048592 | tf_op jit(solution)/shard_map/all_gather | solution.py:17
  57.9 47.5 %all-gather.8.cloned.1.call-done = f32[2048,256]{1,0:T(8,128)} async-done(((f32[512,256]{1,0:T(8,128)}), f32[2048,256]{1,0:T(8,128)}) %all-gather.8.cloned.1.call-update) | async-done | bytes 2097168 | tf_op jit(solution)/shard_map/all_gather | solution.py:17
  105.5 10.3 %while.49 = (s32[]{:T(128)}, f32[512,256]{1,0:T(8,128)S(1)}, f32[512,128]{1,0:T(8,128)S(1)}, f32[1]{0:T(128)}, s32[]{:T(128)}, /*index=5*/f32[4,512,256]{2,1,0:T...) while((s32[]{:T(128)}, f32[512,256]{1,0:T(8,128)S(1)}, ...), condition=%wide.region_4.6_spmd, body=%wide.region_3.5_spmd.sunk | while | flops 196615 | bytes 2359491 | solution.py:26
  119.0 12.8 %collective-permute-done = f32[512,256]{1,0:T(8,128)S(1)} collective-permute-done((f32[512,256]{1,0:T(8,128)S(1)}, f32[512,256]{1,0:T(8,128)S(1)}, u32[]{:S(2)}, u32[]{:S(2)}) %collective-permute-start) | collective-permute-done | bytes 524320 | tf_op jit(solution)/shard_map/ppermute | solution.py:104
  132.3 10.6 %collective-permute-done.2 = f32[512,256]{1,0:T(8,128)S(1)} collective-permute-done((f32[512,256]{1,0:T(8,128)S(1)}, f32[512,256]{1,0:T(8,128)S(1)}, u32[]{:S(2)}, u32[]{:S(2)}) %collective-permute-start.2) | collective-permute-done | bytes 524320 | tf_op jit(solution)/shard_map/ppermute | solution.py:106
  143.0 10.1 %collective-permute-done.1 = f32[512,256]{1,0:T(8,128)S(1)} collective-permute-done((f32[512,256]{1,0:T(8,128)S(1)}, f32[512,256]{1,0:T(8,128)S(1)}, u32[]{:S(2)}, u32[]{:S(2)}) %collective-permute-start.1) | collective-permute-done | bytes 524320 | tf_op jit(solution)/shard_map/ppermute | solution.py:104
  172.3 706.2 %while.51 = (s32[]{:T(128)}, f32[2,1024,128]{2,1,0:T(8,128)}, f32[2,128]{1,0:T(2,128)S(1)}, f32[]{:T(128)}, f32[1024,1024]{0,1:T(8,128)}, /*index=5*/f32[2]{0:T(...) while((s32[]{:T(128)}, f32[2,1024,128]{2,1,0:T(8,128)}, ...), condition=%wide.region_23.25_spmd.clone, body=%wide.region_5.0_spmd.clone.sunk | while | flops 5452662272 | bytes 122106424 | solution.py:66
  191.3 11.7 %cholesky.1066 = f32[128,128]{1,0:T(8,128)S(1)} custom-call(f32[128,128]{1,0:T(8,128)S(1)} %cholesky.1065), custom_call_target="Cholesky" | custom-call | tf_op jit(solution)/shard_map/while/body/eval_jaxpr/jit(cholesky)/cholesky | solution.py:55
  203.0 9.8 %custom-call.142 = f32[1,128,128]{1,2,0:T(8,128)S(1)} custom-call(f32[1,128,128]{2,1,0:T(8,128)S(1)} %get-tuple-element.722), custom_call_target="InvertDiagBlocksLowerTriangular" | custom-call | tf_op jit(solution)/shard_map/while/body/eval_jaxpr/jit(cholesky)/cholesky | solution.py:55
  219.2 12.3 %cholesky.1069 = f32[128,128]{1,0:T(8,128)S(1)} custom-call(f32[128,128]{1,0:T(8,128)S(1)} %cholesky.1068), custom_call_target="Cholesky" | custom-call | tf_op jit(solution)/shard_map/while/body/eval_jaxpr/jit(cholesky)/cholesky | solution.py:55
  247.2 11.7 %cholesky.1071 = f32[128,128]{1,0:T(8,128)S(1)} custom-call(f32[128,128]{1,0:T(8,128)S(1)} %cholesky.1070), custom_call_target="Cholesky" | custom-call | tf_op jit(solution)/shard_map/while/body/eval_jaxpr/jit(cholesky)/cholesky | solution.py:55
  274.2 11.9 %cholesky.1073 = f32[128,128]{1,0:T(8,128)S(1)} custom-call(f32[128,128]{1,0:T(8,128)S(1)} %cholesky.1072), custom_call_target="Cholesky" | custom-call | tf_op jit(solution)/shard_map/while/body/eval_jaxpr/jit(cholesky)/cholesky | solution.py:55
  301.3 11.7 %cholesky.1075 = f32[128,128]{1,0:T(8,128)S(1)} custom-call(f32[128,128]{1,0:T(8,128)S(1)} %cholesky.1074), custom_call_target="Cholesky" | custom-call | tf_op jit(solution)/shard_map/while/body/eval_jaxpr/jit(cholesky)/cholesky | solution.py:55
  315.0 10.0 %custom-call.146 = f32[1,128,128]{1,2,0:T(8,128)S(1)} custom-call(f32[1,128,128]{2,1,0:T(8,128)S(1)} %get-tuple-element.732), custom_call_target="InvertDiagBlocksLowerTriangular" | custom-call | tf_op jit(solution)/shard_map/while/body/eval_jaxpr/jit(cholesky)/cholesky | solution.py:55
  328.2 11.7 %cholesky.1077 = f32[128,128]{1,0:T(8,128)S(1)} custom-call(f32[128,128]{1,0:T(8,128)S(1)} %cholesky.1076), custom_call_target="Cholesky" | custom-call | tf_op jit(solution)/shard_map/while/body/eval_jaxpr/jit(cholesky)/cholesky | solution.py:55
  354.7 12.1 %cholesky.1079 = f32[128,128]{1,0:T(8,128)S(1)} custom-call(f32[128,128]{1,0:T(8,128)S(1)} %cholesky.1078), custom_call_target="Cholesky" | custom-call | tf_op jit(solution)/shard_map/while/body/eval_jaxpr/jit(cholesky)/cholesky | solution.py:55
  381.2 11.7 %cholesky.1080 = f32[128,128]{1,0:T(8,128)S(1)} custom-call(f32[128,128]{1,0:T(8,128)S(1)} %convolution_subtract_fusion.48), custom_call_target="Cholesky" | custom-call | tf_op jit(solution)/shard_map/while/body/eval_jaxpr/jit(cholesky)/cholesky | solution.py:55
  399.7 27.4 %while.52 = (s32[]{:T(128)}, f32[1024,1024]{1,0:T(8,128)}, s32[8,2]{0,1:T(2,128)S(1)}, f32[8,128,128]{2,1,0:T(8,128)}, s32[]{:T(128)}) while((s32[]{:T(128)}, f32[1024,1024]{1,0:T(8,128)}, s32[8,2]{0,1:T(2,128)S(1)}, f32[8,128,128]{2,1,0:T(8,128)}, s32[]{:T(128)}) %tuple.173), condition=%wide.while_cond, body=%wide.while_body.sunk | while | flops 2 | bytes 132705 | solution.py:59
  427.1 79.6 %custom-call.150 = f32[8,128,128]{1,2,0:T(8,128)S(1)} custom-call(f32[8,128,128]{2,1,0:T(8,128)} %get-tuple-element.748), custom_call_target="InvertDiagBlocksLowerTriangular" | custom-call | tf_op jit(solution)/shard_map/while/body/eval_jaxpr/triangular_solve | solution.py:59
  544.0 11.7 %cholesky.1066 = f32[128,128]{1,0:T(8,128)S(1)} custom-call(f32[128,128]{1,0:T(8,128)S(1)} %cholesky.1065), custom_call_target="Cholesky" | custom-call | tf_op jit(solution)/shard_map/while/body/eval_jaxpr/jit(cholesky)/cholesky | solution.py:55
  555.7 9.8 %custom-call.142 = f32[1,128,128]{1,2,0:T(8,128)S(1)} custom-call(f32[1,128,128]{2,1,0:T(8,128)S(1)} %get-tuple-element.722), custom_call_target="InvertDiagBlocksLowerTriangular" | custom-call | tf_op jit(solution)/shard_map/while/body/eval_jaxpr/jit(cholesky)/cholesky | solution.py:55
  571.9 11.9 %cholesky.1069 = f32[128,128]{1,0:T(8,128)S(1)} custom-call(f32[128,128]{1,0:T(8,128)S(1)} %cholesky.1068), custom_call_target="Cholesky" | custom-call | tf_op jit(solution)/shard_map/while/body/eval_jaxpr/jit(cholesky)/cholesky | solution.py:55
  599.5 11.7 %cholesky.1071 = f32[128,128]{1,0:T(8,128)S(1)} custom-call(f32[128,128]{1,0:T(8,128)S(1)} %cholesky.1070), custom_call_target="Cholesky" | custom-call | tf_op jit(solution)/shard_map/while/body/eval_jaxpr/jit(cholesky)/cholesky | solution.py:55
  626.5 11.9 %cholesky.1073 = f32[128,128]{1,0:T(8,128)S(1)} custom-call(f32[128,128]{1,0:T(8,128)S(1)} %cholesky.1072), custom_call_target="Cholesky" | custom-call | tf_op jit(solution)/shard_map/while/body/eval_jaxpr/jit(cholesky)/cholesky | solution.py:55
  653.6 11.7 %cholesky.1075 = f32[128,128]{1,0:T(8,128)S(1)} custom-call(f32[128,128]{1,0:T(8,128)S(1)} %cholesky.1074), custom_call_target="Cholesky" | custom-call | tf_op jit(solution)/shard_map/while/body/eval_jaxpr/jit(cholesky)/cholesky | solution.py:55
  667.3 10.2 %custom-call.146 = f32[1,128,128]{1,2,0:T(8,128)S(1)} custom-call(f32[1,128,128]{2,1,0:T(8,128)S(1)} %get-tuple-element.732), custom_call_target="InvertDiagBlocksLowerTriangular" | custom-call | tf_op jit(solution)/shard_map/while/body/eval_jaxpr/jit(cholesky)/cholesky | solution.py:55
  680.8 11.7 %cholesky.1077 = f32[128,128]{1,0:T(8,128)S(1)} custom-call(f32[128,128]{1,0:T(8,128)S(1)} %cholesky.1076), custom_call_target="Cholesky" | custom-call | tf_op jit(solution)/shard_map/while/body/eval_jaxpr/jit(cholesky)/cholesky | solution.py:55
  707.2 11.9 %cholesky.1079 = f32[128,128]{1,0:T(8,128)S(1)} custom-call(f32[128,128]{1,0:T(8,128)S(1)} %cholesky.1078), custom_call_target="Cholesky" | custom-call | tf_op jit(solution)/shard_map/while/body/eval_jaxpr/jit(cholesky)/cholesky | solution.py:55
  733.5 11.7 %cholesky.1080 = f32[128,128]{1,0:T(8,128)S(1)} custom-call(f32[128,128]{1,0:T(8,128)S(1)} %convolution_subtract_fusion.48), custom_call_target="Cholesky" | custom-call | tf_op jit(solution)/shard_map/while/body/eval_jaxpr/jit(cholesky)/cholesky | solution.py:55
  752.0 27.4 %while.52 = (s32[]{:T(128)}, f32[1024,1024]{1,0:T(8,128)}, s32[8,2]{0,1:T(2,128)S(1)}, f32[8,128,128]{2,1,0:T(8,128)}, s32[]{:T(128)}) while((s32[]{:T(128)}, f32[1024,1024]{1,0:T(8,128)}, s32[8,2]{0,1:T(2,128)S(1)}, f32[8,128,128]{2,1,0:T(8,128)}, s32[]{:T(128)}) %tuple.173), condition=%wide.while_cond, body=%wide.while_body.sunk | while | flops 2 | bytes 132705 | solution.py:59
  779.3 79.6 %custom-call.150 = f32[8,128,128]{1,2,0:T(8,128)S(1)} custom-call(f32[8,128,128]{2,1,0:T(8,128)} %get-tuple-element.748), custom_call_target="InvertDiagBlocksLowerTriangular" | custom-call | tf_op jit(solution)/shard_map/while/body/eval_jaxpr/triangular_solve | solution.py:59
  (348 shorter events, 351.9 us)
Async XLA Ops:
  7.2 18.7 %copy-start.8 = (bf16[1,512,128]{2,1,0:T(8,128)(2,1)S(1)}, bf16[1,512,128]{2,1,0:T(8,128)(2,1)}, u32[]{:S(2)}) copy-start(bf16[1,512,128]{2,1,0:T(8,128)(2,1)} %param.15) | copy-start | bytes 393220
  7.2 50.7 %all-gather.10.cloned.1.call-start = ((), (), s32[]{:S(2)}) async-start(), calls=%async_computation.2 | async-start | bytes 1310720 | tf_op jit(solution)/shard_map/all_gather | solution.py:17
  24.5 3.8 copy-start.12
  25.8 79.6 %copy-start.2 = (bf16[512,1024]{0,1:T(8,128)(2,1)}, bf16[512,1024]{0,1:T(8,128)(2,1)S(1)}, u32[]{:S(2)}) copy-start(bf16[512,1024]{0,1:T(8,128)(2,1)S(1)} %reshape.245) | copy-start | bytes 3145732
  27.1 78.3 %all-gather.8.cloned.1.call-start = ((), (), s32[]{:S(2)}) async-start(), calls=%async_computation.1 | async-start | bytes 2621440 | tf_op jit(solution)/shard_map/all_gather | solution.py:17
  28.3 144.1 %all-gather.6.cloned.1.call-start = ((), (), s32[]{:S(2)}) async-start(), calls=%async_computation | async-start | bytes 6291456 | tf_op jit(solution)/shard_map/all_gather | solution.py:112
  116.0 15.8 %collective-permute-start = (f32[512,256]{1,0:T(8,128)S(1)}, f32[512,256]{1,0:T(8,128)S(1)}, u32[]{:S(2)}, u32[]{:S(2)}) collective-permute-start(f32[512,256]{1,0:T(8,128)S(1)} %add.202), channel_id=1, source_target_pairs={{0,1},{1,2},{2,3},{3,0},{4,5},{5,6},{6,7},{7,4},{8,9},{9,10},{10,1... | collective-permute-start | bytes 1572872 | tf_op jit(solution)/shard_map/ppermute | solution.py:104
  117.5 25.5 %collective-permute-start.2 = (f32[512,256]{1,0:T(8,128)S(1)}, f32[512,256]{1,0:T(8,128)S(1)}, u32[]{:S(2)}, u32[]{:S(2)}) collective-permute-start(f32[512,256]{1,0:T(8,128)S(1)} %add.202), channel_id=1, source_target_pairs={{1,0},{2,1},{3,2},{0,3},{5,4},{6,5},{7,6},{4,7},{9,8},{10,9},{11,1... | collective-permute-start | bytes 1572872 | tf_op jit(solution)/shard_map/ppermute | solution.py:106
  131.7 21.3 %copy-start.3 = (f32[512,256]{1,0:T(8,128)}, f32[512,256]{1,0:T(8,128)S(1)}, u32[]{:S(2)}) copy-start(f32[512,256]{1,0:T(8,128)S(1)} %collective-permute-done) | copy-start | bytes 1572868
  131.8 21.3 %collective-permute-start.1 = (f32[512,256]{1,0:T(8,128)S(1)}, f32[512,256]{1,0:T(8,128)S(1)}, u32[]{:S(2)}, u32[]{:S(2)}) collective-permute-start(f32[512,256]{1,0:T(8,128)S(1)} %collective-permute-done), channel_id=1, source_target_pairs={{0,1},{1,2},{2,3},{3,0},{4,5},{5,6},{6,7},{7,4},{8,9},{9,10},{10,1... | collective-permute-start | bytes 1572872 | tf_op jit(solution)/shard_map/ppermute | solution.py:104
  143.0 10.1 %copy-start.4 = (f32[512,256]{1,0:T(8,128)}, f32[512,256]{1,0:T(8,128)S(1)}, u32[]{:S(2)}) copy-start(f32[512,256]{1,0:T(8,128)S(1)} %collective-permute-done.2) | copy-start | bytes 1572868
  153.1 0.8 copy-start.5
  157.5 4.5 copy-start.10
  157.5 4.5 copy-start.11
  189.3 2.0 copy-start.1
  506.6 8.2 copy-start
  517.6 5.2 copy-start.6
  522.9 2.0 copy-start.7
  542.0 2.0 copy-start.1
  859.0 8.2 copy-start
  869.9 5.2 copy-start.6
  875.2 2.0 copy-start.7
  878.5 1.9 copy-start.9
Sparse Core Ops, SparseCore 0:
  27.2 30.6 all-gather.9
  60.0 45.3 all-gather.7
  160.6 11.6 all-gather.5
